TPU v7x, 256 devices: a whole 4x4x8 slice. The times are simulated.
256 devices in a mesh: row: 32 (over z, x), col: 8 (over y, core).
Axes of the slice: x: 4, y: 4, z: 8, core: 2. Of those that a mesh axis runs over, the one named last changes fastest.
Arguments:
- image: bfloat16 [512, 1024, 256], P('row', 'col'), may hold values from -6 to 6
- kernel_one: bfloat16 [3, 3, 256, 256], replicated, may hold values from -0.125 to 0.125
- kernel_two: bfloat16 [3, 3, 256, 512], replicated, may hold values from -0.125 to 0.125
- cotangent: bfloat16 [256, 512, 512], P('row', 'col'), may hold values from -6 to 6
Outputs:
- image_grad: bfloat16 [512, 1024, 256], P('row', 'col')
- update_one: bfloat16 [3, 3, 256, 256], replicated
- update_two: bfloat16 [3, 3, 256, 512], replicated
All inputs are finite; a program needn't handle non-finite values.
Results may differ from a plain program's by a relative error of at most 0.006.
Values may be sent and summed in bfloat16 or wider, within the bound.
A program may use at most 128 MiB of HBM per device.

v0:
```python
import jax
import jax.numpy as jnp
from jax import lax
from jax.sharding import PartitionSpec as P


def padded(shard, sides, width):
    for axis, dim in sides:
        size, length = (lax.axis_size(axis), shard.shape[dim])
        up = [(i, (i + 1) % size) for i in range(size - 1)]
        down = [(j, i) for i, j in up]
        last = lax.slice_in_dim(shard, length - width, length, axis=dim)
        initial = lax.slice_in_dim(shard, 0, width, axis=dim)
        before = lax.ppermute(last, axis, up)
        after = lax.ppermute(initial, axis, down)
        shard = jnp.concatenate([before, shard, after], axis=dim)
    return shard


def passed_along(shard, axis, by):
    size = lax.axis_size(axis)
    pairs = [(i, i + by) for i in range(size) if 0 <= i + by < size]
    return lax.ppermute(shard, axis, pairs)


def conv_local(source, kernel, padding, dilation, layout):
    result = lax.conv_general_dilated(
        source[None],
        kernel,
        (1, 1),
        padding,
        lhs_dilation=dilation,
        dimension_numbers=("NHWC", layout, "NHWC"),
        preferred_element_type=jnp.float32,
    )
    return result[0]


def on_device(image, kernel_one, kernel_two, cotangent):
    rows_here = image.shape[0]
    cols_here = image.shape[1]
    image_pad = padded(image, (("row", 0), ("col", 1)), 1)
    pre_act = conv_local(image_pad, kernel_one, "VALID", (1, 1), "HWIO")
    activ = jax.nn.silu(pre_act).astype(jnp.bfloat16)
    left_edge = passed_along(activ[:, -1:], "col", 1)
    act_cols = jnp.concatenate([left_edge, activ], 1)
    top_edge = passed_along(act_cols[-1:], "row", 1)
    act_pad = jnp.concatenate([top_edge, act_cols], 0)
    rows_two = []
    for row_off in range(3):
        cols_two = []
        for col_off in range(3):
            patch = act_pad[
                row_off : row_off + rows_here - 1 : 2, col_off : col_off + cols_here - 1 : 2
            ]
            cols_two.append(
                jnp.einsum("ijc,ije->ce", patch, cotangent, preferred_element_type=jnp.float32)
            )
        rows_two.append(jnp.stack(cols_two))
    grad_two = jnp.stack(rows_two)
    flipped_two = kernel_two[::-1, ::-1]
    act_full = conv_local(cotangent, flipped_two, ((2, 2), (2, 2)), (2, 2), "HWOI")
    from_right = passed_along(act_full[:, :1], "col", -1)
    act_trim = act_full[:, 1:]
    act_trim = jnp.concatenate([act_trim[:, :-1], act_trim[:, -1:] + from_right], 1)
    from_below = passed_along(act_trim[:1].astype(jnp.bfloat16), "row", -1).astype(jnp.float32)
    act_grad = act_trim[1:]
    act_grad = jnp.concatenate([act_grad[:-1], act_grad[-1:] + from_below], 0)
    sig = jax.nn.sigmoid(pre_act)
    pre_grad = (act_grad * sig * (1.0 + pre_act * (1.0 - sig))).astype(jnp.bfloat16)
    rows_one = []
    for row_off in range(3):
        cols_one = []
        for col_off in range(3):
            patch = image_pad[row_off : row_off + rows_here, col_off : col_off + cols_here]
            cols_one.append(
                jnp.einsum("ijc,ijd->cd", patch, pre_grad, preferred_element_type=jnp.float32)
            )
        rows_one.append(jnp.stack(cols_one))
    grad_one = jnp.stack(rows_one)
    grad_pad = padded(pre_grad, (("row", 0), ("col", 1)), 1)
    image_grad = conv_local(grad_pad, kernel_one[::-1, ::-1], "VALID", (1, 1), "HWOI").astype(
        jnp.bfloat16
    )
    flat_one = grad_one.reshape(-1)
    flat_two = grad_two.reshape(-1)
    total_one, total_two = lax.psum((flat_one, flat_two), ("row", "col"))
    update_one = (total_one * lax.rsqrt(jnp.mean(total_one * total_one) + 1e-06)).astype(
        jnp.bfloat16
    )
    update_two = (total_two * lax.rsqrt(jnp.mean(total_two * total_two) + 1e-06)).astype(
        jnp.bfloat16
    )
    return (image_grad, update_one.reshape(kernel_one.shape), update_two.reshape(kernel_two.shape))


def solution(mesh):
    placed = (P("row", "col", None), P(), P(), P("row", "col", None))
    return jax.shard_map(
        on_device,
        mesh=mesh,
        in_specs=placed,
        out_specs=(P("row", "col", None), P(), P()),
        check_vma=False,
    )
```

profile of v0, /device:TPU:2, one launch (start us, length us, event | category | flops | bytes accessed | tf_op | source)
XLA Modules:
  0.0 440.2 jit_solution(7343728317577428346)
XLA Ops:
  13.3 4.1 reshape.29
  22.8 3.4 collective-permute-start.2
  47.9 4.4 maximum_bitcast_fusion
  52.3 3.9 copy.64
  58.6 3.2 reshape.32
  63.8 3.0 convolution_select_fusion.1
  66.9 3.6 maximum_maximum_fusion
  74.7 2.7 slice.143
  80.1 2.7 slice.146
  82.8 2.7 slice.145
  91.0 4.4 %collective-permute-start.10 = (bf16[16,1,256]{2,1,0:T(2,128)(2,1)S(1)}, bf16[16,1,256]{2,1,0:T(2,128)(2,1)S(1)}, u32[]{:S(2)}, u32[]{:S(2)}) collective-permute-start(bf16[16,1,256]{2,1,0:T(2,128)(2,1)S(1)} %slice.178), channel_id=1, source_target_pairs={{0,1},{1,2},{2,3},{3,4},{4,5},{5,6},{6,7},{8,9},{9,10},{10,11},{11... | collective-permute-start | bytes 24584 | tf_op jit(solution)/shard_map/ppermute | solution.py:23
  104.3 2.7 slice.141
  107.5 3.8 collective-permute-start.11
  115.7 2.7 slice.140
  118.4 2.7 slice.139
  127.9 3.4 copy.66
  131.3 4.7 %collective-permute-start.6 = (bf16[1,128,256]{2,1,0:T(8,128)(2,1)S(1)}, bf16[1,128,256]{2,1,0:T(8,128)(2,1)S(1)}, u32[]{:S(2)}, u32[]{:S(2)}) collective-permute-start(bf16[1,128,256]{2,1,0:T(8,128)(2,1)S(1)} %get-tuple-element.19), channel_id=1, source_target_pairs={{0,8},{8,16},{16,24},{24,32},{32,40},{40,48},{48,56},{56,64},{64,7... | collective-permute-start | bytes 196616 | tf_op jit(solution)/shard_map/ppermute | solution.py:14
  138.0 5.9 %collective-permute-done.7 = bf16[1,128,256]{2,1,0:T(8,128)(2,1)S(1)} collective-permute-done((bf16[1,128,256]{2,1,0:T(8,128)(2,1)S(1)}, bf16[1,128,256]{2,1,0:T(8,128)(2,1)S(1)}, u32[]{:S(2)}, u32[]{:S(2)}) %collective-permute-start.7) | collective-permute-done | bytes 65568 | tf_op jit(solution)/shard_map/ppermute | solution.py:15
  148.0 3.1 collective-permute-done.9
  156.7 2.8 select_convert_fusion
  161.1 255.9 %all-reduce.3.cloned.1.call-done = (f32[589824]{0:T(1024)}, f32[1179648]{0:T(1024)}) async-done(((f32[589824]{0:T(1024)}, f32[1179648]{0:T(1024)}), (f32[589824]{0:T(1024)}, f32[1179648]{0:T(1024)})) %all-reduce.3.cloned.1.call-update) | async-done | bytes 7077904 | tf_op jit(solution)/shard_map/psum | solution.py:87
  417.1 3.6 multiply_reduce_fusion
  423.9 2.7 reshape.22
  426.6 2.9 multiply_reduce_fusion.1
  (148 shorter events, 89.0 us)
Async XLA Ops:
  7.2 409.9 %all-reduce.3.cloned.1.call-start = ((), (), s32[]{:S(2)}) async-start(), calls=%async_computation | async-start | bytes 14155776 | tf_op jit(solution)/shard_map/psum | solution.py:87
  17.4 4.7 %copy-start.9 = (bf16[16,128,256]{2,1,0:T(8,128)(2,1)S(1)}, bf16[16,128,256]{2,1,0:T(8,128)(2,1)}, u32[]{:S(2)}) copy-start(bf16[16,128,256]{2,1,0:T(8,128)(2,1)} %param.4) | copy-start | bytes 3145732
  20.8 9.8 %collective-permute-start = (f32[17,1,256]{2,1,0:T(1,128)S(1)}, f32[17,1,256]{2,1,0:T(1,128)S(1)}, u32[]{:S(2)}, u32[]{:S(2)}) collective-permute-start(f32[17,1,256]{2,1,0:T(1,128)S(1)} %slice.157), channel_id=1, source_target_pairs={{1,0},{2,1},{3,2},{4,3},{5,4},{6,5},{7,6},{9,8},{10,9},{11,10},{12... | collective-permute-start | bytes 52232 | tf_op jit(solution)/shard_map/ppermute | solution.py:23
  22.8 10.2 %collective-permute-start.2 = (bf16[1,128,256]{1,2,0:T(8,128)(2,1)S(1)}, bf16[1,128,256]{1,2,0:T(8,128)(2,1)S(1)}, u32[]{:S(2)}, u32[]{:S(2)}) collective-permute-start(bf16[1,128,256]{1,2,0:T(8,128)(2,1)S(1)} %get-tuple-element.21), channel_id=1, source_target_pairs={{0,8},{8,16},{16,24},{24,32},{32,40},{40,48},{48,56},{56,64},{64,7... | collective-permute-start | bytes 196616 | tf_op jit(solution)/shard_map/ppermute | solution.py:14
  26.2 6.8 %collective-permute-start.3 = (bf16[1,128,256]{1,2,0:T(8,128)(2,1)S(1)}, bf16[1,128,256]{1,2,0:T(8,128)(2,1)S(1)}, u32[]{:S(2)}, u32[]{:S(2)}) collective-permute-start(bf16[1,128,256]{1,2,0:T(8,128)(2,1)S(1)} %get-tuple-element.22), channel_id=1, source_target_pairs={{8,0},{16,8},{24,16},{32,24},{40,32},{48,40},{56,48},{64,56},{72,6... | collective-permute-start | bytes 196616 | tf_op jit(solution)/shard_map/ppermute | solution.py:15
  36.8 8.1 %collective-permute-start.4 = (bf16[18,1,256]{2,0,1:T(8,128)(2,1)S(1)}, bf16[18,1,256]{2,0,1:T(8,128)(2,1)S(1)}, u32[]{:S(2)}, u32[]{:S(2)}) collective-permute-start(bf16[18,1,256]{2,0,1:T(8,128)(2,1)S(1)} %copy.41), channel_id=1, source_target_pairs={{0,1},{1,2},{2,3},{3,4},{4,5},{5,6},{6,7},{8,9},{9,10},{10,11},{11... | collective-permute-start | bytes 27656 | tf_op jit(solution)/shard_map/ppermute | solution.py:14
  41.1 5.4 %collective-permute-start.5 = (bf16[18,1,256]{2,0,1:T(8,128)(2,1)S(1)}, bf16[18,1,256]{2,0,1:T(8,128)(2,1)S(1)}, u32[]{:S(2)}, u32[]{:S(2)}) collective-permute-start(bf16[18,1,256]{2,0,1:T(8,128)(2,1)S(1)} %copy.42), channel_id=1, source_target_pairs={{1,0},{2,1},{3,2},{4,3},{5,4},{6,5},{7,6},{9,8},{10,9},{11,10},{12... | collective-permute-start | bytes 27656 | tf_op jit(solution)/shard_map/ppermute | solution.py:15
  43.1 28.3 %collective-permute-start.1 = (bf16[1,128,256]{2,1,0:T(8,128)(2,1)}, bf16[1,128,256]{2,1,0:T(8,128)(2,1)S(1)}, u32[]{:S(2)}, u32[]{:S(2)}) collective-permute-start(bf16[1,128,256]{2,1,0:T(8,128)(2,1)} %fusion.41), channel_id=1, source_target_pairs={{8,0},{16,8},{24,16},{32,24},{40,32},{48,40},{56,48},{64,56},{72,6... | collective-permute-start | bytes 196616 | tf_op jit(solution)/shard_map/ppermute | solution.py:23
  90.0 5.5 %copy-start.14 = (bf16[8,64,512]{2,1,0:T(8,128)(2,1)S(1)}, bf16[8,64,512]{2,1,0:T(8,128)(2,1)}, u32[]{:S(2)}) copy-start(bf16[8,64,512]{2,1,0:T(8,128)(2,1)} %param.7) | copy-start | bytes 1572868
  90.0 5.5 %copy-start.21 = (bf16[8,64,256]{2,1,0:T(8,128)(2,1)S(1)}, bf16[8,64,256]{2,1,0:T(8,128)(2,1)}, u32[]{:S(2)}) copy-start(bf16[8,64,256]{2,1,0:T(8,128)(2,1)} %slice.143) | copy-start | bytes 786436
  90.4 6.2 %copy-start.20 = (bf16[8,64,256]{2,1,0:T(8,128)(2,1)S(1)}, bf16[8,64,256]{2,1,0:T(8,128)(2,1)}, u32[]{:S(2)}) copy-start(bf16[8,64,256]{2,1,0:T(8,128)(2,1)} %slice.142) | copy-start | bytes 786436
  91.0 6.8 %copy-start.19 = (bf16[8,64,256]{2,1,0:T(8,128)(2,1)S(1)}, bf16[8,64,256]{2,1,0:T(8,128)(2,1)}, u32[]{:S(2)}) copy-start(bf16[8,64,256]{2,1,0:T(8,128)(2,1)} %slice.146) | copy-start | bytes 786436
  91.0 7.9 %copy-start.18 = (bf16[8,64,256]{2,1,0:T(8,128)(2,1)S(1)}, bf16[8,64,256]{2,1,0:T(8,128)(2,1)}, u32[]{:S(2)}) copy-start(bf16[8,64,256]{2,1,0:T(8,128)(2,1)} %slice.145) | copy-start | bytes 786436
  91.0 12.9 %collective-permute-start.10 = (bf16[16,1,256]{2,1,0:T(2,128)(2,1)S(1)}, bf16[16,1,256]{2,1,0:T(2,128)(2,1)S(1)}, u32[]{:S(2)}, u32[]{:S(2)}) collective-permute-start(bf16[16,1,256]{2,1,0:T(2,128)(2,1)S(1)} %slice.178), channel_id=1, source_target_pairs={{0,1},{1,2},{2,3},{3,4},{4,5},{5,6},{6,7},{8,9},{9,10},{10,11},{11... | collective-permute-start | bytes 24584 | tf_op jit(solution)/shard_map/ppermute | solution.py:23
  103.9 9.7 %copy-start.22 = (bf16[16,1,256]{2,1,0:T(2,128)(2,1)}, bf16[16,1,256]{2,1,0:T(2,128)(2,1)S(1)}, u32[]{:S(2)}) copy-start(bf16[16,1,256]{2,1,0:T(2,128)(2,1)S(1)} %collective-permute-done.10) | copy-start | bytes 24580
  107.5 6.1 %copy-start.15 = (bf16[8,64,512]{2,1,0:T(8,128)(2,1)S(1)}, bf16[8,64,512]{2,1,0:T(8,128)(2,1)}, u32[]{:S(2)}) copy-start(bf16[8,64,512]{2,1,0:T(8,128)(2,1)} %param.7) | copy-start | bytes 1572868
  107.5 6.4 %copy-start.16 = (f32[1,256,512]{2,1,0:T(8,128)S(1)}, f32[1,256,512]{2,1,0:T(8,128)}, u32[]{:S(2)}) copy-start(f32[1,256,512]{2,1,0:T(8,128)} %convolution_bitcast_fusion) | copy-start | bytes 1572868
  107.5 6.4 %copy-start.17 = (f32[1,256,512]{2,1,0:T(8,128)S(1)}, f32[1,256,512]{2,1,0:T(8,128)}, u32[]{:S(2)}) copy-start(f32[1,256,512]{2,1,0:T(8,128)} %convolution_bitcast_fusion.1) | copy-start | bytes 1572868
  107.5 7.7 %collective-permute-start.11 = (bf16[1,129,256]{2,1,0:T(8,128)(2,1)S(1)}, bf16[1,129,256]{2,1,0:T(8,128)(2,1)S(1)}, u32[]{:S(2)}, u32[]{:S(2)}) collective-permute-start(bf16[1,129,256]{2,1,0:T(8,128)(2,1)S(1)} %fusion.42), channel_id=1, source_target_pairs={{0,8},{8,16},{16,24},{24,32},{32,40},{40,48},{48,56},{56,64},{64,7... | collective-permute-start | bytes 198152 | tf_op jit(solution)/shard_map/ppermute | solution.py:23
  121.5 4.4 copy-start.11
  131.3 6.7 %collective-permute-start.6 = (bf16[1,128,256]{2,1,0:T(8,128)(2,1)S(1)}, bf16[1,128,256]{2,1,0:T(8,128)(2,1)S(1)}, u32[]{:S(2)}, u32[]{:S(2)}) collective-permute-start(bf16[1,128,256]{2,1,0:T(8,128)(2,1)S(1)} %get-tuple-element.19), channel_id=1, source_target_pairs={{0,8},{8,16},{16,24},{24,32},{32,40},{40,48},{48,56},{56,64},{64,7... | collective-permute-start | bytes 196616 | tf_op jit(solution)/shard_map/ppermute | solution.py:14
  135.9 8.0 %collective-permute-start.7 = (bf16[1,128,256]{2,1,0:T(8,128)(2,1)S(1)}, bf16[1,128,256]{2,1,0:T(8,128)(2,1)S(1)}, u32[]{:S(2)}, u32[]{:S(2)}) collective-permute-start(bf16[1,128,256]{2,1,0:T(8,128)(2,1)S(1)} %get-tuple-element.20), channel_id=1, source_target_pairs={{8,0},{16,8},{24,16},{32,24},{40,32},{48,40},{56,48},{64,56},{72,6... | collective-permute-start | bytes 196616 | tf_op jit(solution)/shard_map/ppermute | solution.py:15
  143.9 4.1 collective-permute-start.8
  146.4 4.7 %collective-permute-start.9 = (bf16[18,1,256]{2,1,0:T(2,128)(2,1)S(1)}, bf16[18,1,256]{2,1,0:T(2,128)(2,1)S(1)}, u32[]{:S(2)}, u32[]{:S(2)}) collective-permute-start(bf16[18,1,256]{2,1,0:T(2,128)(2,1)S(1)} %get-tuple-element.16), channel_id=1, source_target_pairs={{1,0},{2,1},{3,2},{4,3},{5,4},{6,5},{7,6},{9,8},{10,9},{11,10},{12... | collective-permute-start | bytes 27656 | tf_op jit(solution)/shard_map/ppermute | solution.py:15
  (17 other events, 38.5 us)
Sparse Core Ops, SparseCore 0:
  131.4 285.6 all-reduce.2
where the time goes:
time: 441 us; the launch traced here: 440 us
  waiting for transfers between devices  265 us (60%)
  local copies, waits for them, and re-layouts  74.5 us (17%)
  starting transfers between devices  31.7 us (7%)
  other arithmetic  28 us (6%)
  matrix products  24.6 us (6%)
  between operations  16.2 us (4%)
    psum x1, waiting for transfers between devices, on_device(): total_one, total_two = lax.psum((flat_one, flat_two), ('row', 'col'))  256 us
    slice x9, local copies, waits for them, and re-layouts, on_device(): act_pad[row_off:row_off + rows_here - 1:2, col_off:col_off + cols_here -...  19.8 us
    unnamed x62, local copies, waits for them, and re-layouts  18.9 us
    conv_general_dilated x12, local copies, waits for them, and re-layouts, conv_local(): lax.conv_general_dilated(source[None], kernel, (1, 1), padding, lhs_dilat...  15.6 us
    ppermute x4, starting transfers between devices, padded(): before = lax.ppermute(last, axis, up)  13 us
    dot_general x9, matrix products, on_device(): jnp.einsum('ijc,ije->ce', patch, cotangent, preferred_element_type=jnp.fl...  11.4 us
    ppermute x4, starting transfers between devices, passed_along(): return lax.ppermute(shard, axis, pairs)  11.4 us
    ppermute x4, waiting for transfers between devices, padded(): after = lax.ppermute(initial, axis, down)  9.07 us
  transfers between devices with their start and end apart: 13, of which 4 were waited for; matrix products, arithmetic and copies ran while one was open for 12% of the time, Pallas kernels for 0%

commit v1 on v0

--- a/solution.py
+++ b/solution.py
@@ -84,7 +84,7 @@
     )
     flat_one = grad_one.reshape(-1)
     flat_two = grad_two.reshape(-1)
-    total_one, total_two = lax.psum((flat_one, flat_two), ("row", "col"))
+    total_one, total_two = lax.psum(lax.psum((flat_one, flat_two), "row"), "col")
     update_one = (total_one * lax.rsqrt(jnp.mean(total_one * total_one) + 1e-06)).astype(
         jnp.bfloat16
     )

time: 441 us -> 459 us (1.041)
  waiting for transfers between devices: 265 us -> 284 us
    psum x1 -> x2, waiting for transfers between devices: 256 us -> 277 us  [the longest x1 204 us: on_device(): lax.psum((flat_one, flat_two), 'row')]
  transfers between devices with their start and end apart: 13 -> 14, of which waited for: 4 -> 5; matrix products, arithmetic and copies ran while one was open for 12% -> 12% of each run, Pallas kernels for 0% -> 0%
where the time goes in v1:
time: 459 us; the launch traced here: 457 us
  waiting for transfers between devices  284 us (62%)
  local copies, waits for them, and re-layouts  74.5 us (16%)
  starting transfers between devices  29.8 us (6%)
  other arithmetic  28.1 us (6%)
  matrix products  24.6 us (5%)
  between operations  16.2 us (4%)
    psum x1, waiting for transfers between devices, on_device(): lax.psum((flat_one, flat_two), 'row')  204 us
    psum x1, waiting for transfers between devices, on_device(): lax.psum(lax.psum((flat_one, flat_two), 'row'), 'col')  72.7 us
    slice x9, local copies, waits for them, and re-layouts, on_device(): act_pad[row_off:row_off + rows_here - 1:2, col_off:col_off + cols_here -...  19.8 us
    unnamed x62, local copies, waits for them, and re-layouts  19 us
    conv_general_dilated x12, local copies, waits for them, and re-layouts, conv_local(): lax.conv_general_dilated(source[None], kernel, (1, 1), padding, lhs_dilat...  15.6 us
    dot_general x9, matrix products, on_device(): jnp.einsum('ijc,ije->ce', patch, cotangent, preferred_element_type=jnp.fl...  11.4 us
    ppermute x4, starting transfers between devices, passed_along(): return lax.ppermute(shard, axis, pairs)  11.4 us
    ppermute x4, starting transfers between devices, padded(): before = lax.ppermute(last, axis, up)  10.5 us
  transfers between devices with their start and end apart: 14, of which 5 were waited for; matrix products, arithmetic and copies ran while one was open for 12% of the time, Pallas kernels for 0%

profile of v1, /device:TPU:2, one launch (start us, length us, event | category | flops | bytes accessed | tf_op | source)
XLA Modules:
  0.0 457.1 jit_solution(3779695067258547471)
XLA Ops:
  13.3 4.1 reshape.29
  22.8 3.4 collective-permute-start.2
  48.0 4.4 maximum_bitcast_fusion
  52.3 3.9 copy.64
  58.6 3.2 reshape.32
  63.9 3.0 convolution_select_fusion.1
  66.9 3.6 maximum_maximum_fusion
  80.1 2.7 slice.146
  82.9 2.7 slice.145
  91.1 4.4 collective-permute-start.10
  104.4 2.7 slice.141
  107.6 3.8 collective-permute-start.11
  115.7 2.7 slice.140
  118.5 2.7 slice.139
  127.9 3.4 copy.66
  131.4 204.3 %all-reduce.5.cloned.1.call-done = (f32[589824]{0:T(1024)}, f32[1179648]{0:T(1024)}) async-done(((f32[589824]{0:T(1024)}, f32[1179648]{0:T(1024)}), (f32[589824]{0:T(1024)}, f32[1179648]{0:T(1024)})) %all-reduce.5.cloned.1.call-update) | async-done | bytes 7077904 | tf_op jit(solution)/shard_map/psum | solution.py:87
  335.7 3.4 collective-permute-start.6
  341.9 3.4 collective-permute-done.7
  348.2 3.2 collective-permute-done.9
  356.9 2.8 select_convert_fusion
  361.3 72.7 %all-reduce.7.cloned.1.call-done = (f32[589824]{0:T(1024)}, f32[1179648]{0:T(1024)}) async-done(((f32[589824]{0:T(1024)}, f32[1179648]{0:T(1024)}), (f32[589824]{0:T(1024)}, f32[1179648]{0:T(1024)})) %all-reduce.7.cloned.1.call-update) | async-done | bytes 7077904 | tf_op jit(solution)/shard_map/psum | solution.py:87
  434.0 3.6 multiply_reduce_fusion
  440.8 2.7 reshape.22
  443.5 2.9 multiply_reduce_fusion.1
  (151 shorter events, 91.1 us)
Async XLA Ops:
  7.2 328.5 %all-reduce.5.cloned.1.call-start = ((), (), s32[]{:S(2)}) async-start(), calls=%async_computation | async-start | bytes 14155776 | tf_op jit(solution)/shard_map/psum | solution.py:87
  17.4 4.6 %copy-start.9 = (bf16[16,128,256]{2,1,0:T(8,128)(2,1)S(1)}, bf16[16,128,256]{2,1,0:T(8,128)(2,1)}, u32[]{:S(2)}) copy-start(bf16[16,128,256]{2,1,0:T(8,128)(2,1)} %param.4) | copy-start | bytes 3145732
  20.8 9.8 %collective-permute-start = (f32[17,1,256]{2,1,0:T(1,128)S(1)}, f32[17,1,256]{2,1,0:T(1,128)S(1)}, u32[]{:S(2)}, u32[]{:S(2)}) collective-permute-start(f32[17,1,256]{2,1,0:T(1,128)S(1)} %slice.157), channel_id=1, source_target_pairs={{1,0},{2,1},{3,2},{4,3},{5,4},{6,5},{7,6},{9,8},{10,9},{11,10},{12... | collective-permute-start | bytes 52232 | tf_op jit(solution)/shard_map/ppermute | solution.py:23
  22.8 10.2 %collective-permute-start.2 = (bf16[1,128,256]{1,2,0:T(8,128)(2,1)S(1)}, bf16[1,128,256]{1,2,0:T(8,128)(2,1)S(1)}, u32[]{:S(2)}, u32[]{:S(2)}) collective-permute-start(bf16[1,128,256]{1,2,0:T(8,128)(2,1)S(1)} %get-tuple-element.23), channel_id=1, source_target_pairs={{0,8},{8,16},{16,24},{24,32},{32,40},{40,48},{48,56},{56,64},{64,7... | collective-permute-start | bytes 196616 | tf_op jit(solution)/shard_map/ppermute | solution.py:14
  26.2 6.8 %collective-permute-start.3 = (bf16[1,128,256]{1,2,0:T(8,128)(2,1)S(1)}, bf16[1,128,256]{1,2,0:T(8,128)(2,1)S(1)}, u32[]{:S(2)}, u32[]{:S(2)}) collective-permute-start(bf16[1,128,256]{1,2,0:T(8,128)(2,1)S(1)} %get-tuple-element.24), channel_id=1, source_target_pairs={{8,0},{16,8},{24,16},{32,24},{40,32},{48,40},{56,48},{64,56},{72,6... | collective-permute-start | bytes 196616 | tf_op jit(solution)/shard_map/ppermute | solution.py:15
  36.9 8.1 %collective-permute-start.4 = (bf16[18,1,256]{2,0,1:T(8,128)(2,1)S(1)}, bf16[18,1,256]{2,0,1:T(8,128)(2,1)S(1)}, u32[]{:S(2)}, u32[]{:S(2)}) collective-permute-start(bf16[18,1,256]{2,0,1:T(8,128)(2,1)S(1)} %copy.41), channel_id=1, source_target_pairs={{0,1},{1,2},{2,3},{3,4},{4,5},{5,6},{6,7},{8,9},{9,10},{10,11},{11... | collective-permute-start | bytes 27656 | tf_op jit(solution)/shard_map/ppermute | solution.py:14
  41.1 5.4 %collective-permute-start.5 = (bf16[18,1,256]{2,0,1:T(8,128)(2,1)S(1)}, bf16[18,1,256]{2,0,1:T(8,128)(2,1)S(1)}, u32[]{:S(2)}, u32[]{:S(2)}) collective-permute-start(bf16[18,1,256]{2,0,1:T(8,128)(2,1)S(1)} %copy.42), channel_id=1, source_target_pairs={{1,0},{2,1},{3,2},{4,3},{5,4},{6,5},{7,6},{9,8},{10,9},{11,10},{12... | collective-permute-start | bytes 27656 | tf_op jit(solution)/shard_map/ppermute | solution.py:15
  43.1 28.4 %collective-permute-start.1 = (bf16[1,128,256]{2,1,0:T(8,128)(2,1)}, bf16[1,128,256]{2,1,0:T(8,128)(2,1)S(1)}, u32[]{:S(2)}, u32[]{:S(2)}) collective-permute-start(bf16[1,128,256]{2,1,0:T(8,128)(2,1)} %fusion.41), channel_id=1, source_target_pairs={{8,0},{16,8},{24,16},{32,24},{40,32},{48,40},{56,48},{64,56},{72,6... | collective-permute-start | bytes 196616 | tf_op jit(solution)/shard_map/ppermute | solution.py:23
  90.1 5.5 %copy-start.14 = (bf16[8,64,512]{2,1,0:T(8,128)(2,1)S(1)}, bf16[8,64,512]{2,1,0:T(8,128)(2,1)}, u32[]{:S(2)}) copy-start(bf16[8,64,512]{2,1,0:T(8,128)(2,1)} %param.7) | copy-start | bytes 1572868
  90.1 5.5 %copy-start.21 = (bf16[8,64,256]{2,1,0:T(8,128)(2,1)S(1)}, bf16[8,64,256]{2,1,0:T(8,128)(2,1)}, u32[]{:S(2)}) copy-start(bf16[8,64,256]{2,1,0:T(8,128)(2,1)} %slice.143) | copy-start | bytes 786436
  90.5 6.1 %copy-start.20 = (bf16[8,64,256]{2,1,0:T(8,128)(2,1)S(1)}, bf16[8,64,256]{2,1,0:T(8,128)(2,1)}, u32[]{:S(2)}) copy-start(bf16[8,64,256]{2,1,0:T(8,128)(2,1)} %slice.142) | copy-start | bytes 786436
  91.1 6.7 %copy-start.19 = (bf16[8,64,256]{2,1,0:T(8,128)(2,1)S(1)}, bf16[8,64,256]{2,1,0:T(8,128)(2,1)}, u32[]{:S(2)}) copy-start(bf16[8,64,256]{2,1,0:T(8,128)(2,1)} %slice.146) | copy-start | bytes 786436
  91.1 7.8 %copy-start.18 = (bf16[8,64,256]{2,1,0:T(8,128)(2,1)S(1)}, bf16[8,64,256]{2,1,0:T(8,128)(2,1)}, u32[]{:S(2)}) copy-start(bf16[8,64,256]{2,1,0:T(8,128)(2,1)} %slice.145) | copy-start | bytes 786436
  91.1 12.8 %collective-permute-start.10 = (bf16[16,1,256]{2,1,0:T(2,128)(2,1)S(1)}, bf16[16,1,256]{2,1,0:T(2,128)(2,1)S(1)}, u32[]{:S(2)}, u32[]{:S(2)}) collective-permute-start(bf16[16,1,256]{2,1,0:T(2,128)(2,1)S(1)} %slice.178), channel_id=1, source_target_pairs={{0,1},{1,2},{2,3},{3,4},{4,5},{5,6},{6,7},{8,9},{9,10},{10,11},{11... | collective-permute-start | bytes 24584 | tf_op jit(solution)/shard_map/ppermute | solution.py:23
  103.9 9.7 %copy-start.22 = (bf16[16,1,256]{2,1,0:T(2,128)(2,1)}, bf16[16,1,256]{2,1,0:T(2,128)(2,1)S(1)}, u32[]{:S(2)}) copy-start(bf16[16,1,256]{2,1,0:T(2,128)(2,1)S(1)} %collective-permute-done.10) | copy-start | bytes 24580
  107.5 6.1 %copy-start.15 = (bf16[8,64,512]{2,1,0:T(8,128)(2,1)S(1)}, bf16[8,64,512]{2,1,0:T(8,128)(2,1)}, u32[]{:S(2)}) copy-start(bf16[8,64,512]{2,1,0:T(8,128)(2,1)} %param.7) | copy-start | bytes 1572868
  107.5 6.4 %copy-start.16 = (f32[1,256,512]{2,1,0:T(8,128)S(1)}, f32[1,256,512]{2,1,0:T(8,128)}, u32[]{:S(2)}) copy-start(f32[1,256,512]{2,1,0:T(8,128)} %convolution_bitcast_fusion) | copy-start | bytes 1572868
  107.6 6.4 %copy-start.17 = (f32[1,256,512]{2,1,0:T(8,128)S(1)}, f32[1,256,512]{2,1,0:T(8,128)}, u32[]{:S(2)}) copy-start(f32[1,256,512]{2,1,0:T(8,128)} %convolution_bitcast_fusion.1) | copy-start | bytes 1572868
  107.6 7.7 %collective-permute-start.11 = (bf16[1,129,256]{2,1,0:T(8,128)(2,1)S(1)}, bf16[1,129,256]{2,1,0:T(8,128)(2,1)S(1)}, u32[]{:S(2)}, u32[]{:S(2)}) collective-permute-start(bf16[1,129,256]{2,1,0:T(8,128)(2,1)S(1)} %fusion.42), channel_id=1, source_target_pairs={{0,8},{8,16},{16,24},{24,32},{32,40},{40,48},{48,56},{56,64},{64,7... | collective-permute-start | bytes 198152 | tf_op jit(solution)/shard_map/ppermute | solution.py:23
  131.3 302.7 %all-reduce.7.cloned.1.call-start = ((), (), s32[]{:S(2)}) async-start(), calls=%async_computation.1 | async-start | bytes 14155776 | tf_op jit(solution)/shard_map/psum | solution.py:87
  335.7 6.2 %collective-permute-start.6 = (bf16[1,128,256]{2,1,0:T(8,128)(2,1)S(1)}, bf16[1,128,256]{2,1,0:T(8,128)(2,1)S(1)}, u32[]{:S(2)}, u32[]{:S(2)}) collective-permute-start(bf16[1,128,256]{2,1,0:T(8,128)(2,1)S(1)} %get-tuple-element.21), channel_id=1, source_target_pairs={{0,8},{8,16},{16,24},{24,32},{32,40},{40,48},{48,56},{56,64},{64,7... | collective-permute-start | bytes 196616 | tf_op jit(solution)/shard_map/ppermute | solution.py:14
  339.1 6.2 %collective-permute-start.7 = (bf16[1,128,256]{2,1,0:T(8,128)(2,1)S(1)}, bf16[1,128,256]{2,1,0:T(8,128)(2,1)S(1)}, u32[]{:S(2)}, u32[]{:S(2)}) collective-permute-start(bf16[1,128,256]{2,1,0:T(8,128)(2,1)S(1)} %get-tuple-element.22), channel_id=1, source_target_pairs={{8,0},{16,8},{24,16},{32,24},{40,32},{48,40},{56,48},{64,56},{72,6... | collective-permute-start | bytes 196616 | tf_op jit(solution)/shard_map/ppermute | solution.py:15
  345.3 2.9 collective-permute-start.8
  346.6 4.8 %collective-permute-start.9 = (bf16[18,1,256]{2,1,0:T(2,128)(2,1)S(1)}, bf16[18,1,256]{2,1,0:T(2,128)(2,1)S(1)}, u32[]{:S(2)}, u32[]{:S(2)}) collective-permute-start(bf16[18,1,256]{2,1,0:T(2,128)(2,1)S(1)} %get-tuple-element.18), channel_id=1, source_target_pairs={{1,0},{2,1},{3,2},{4,3},{5,4},{6,5},{7,6},{9,8},{10,9},{11,10},{12... | collective-permute-start | bytes 27656 | tf_op jit(solution)/shard_map/ppermute | solution.py:15
  (18 other events, 42.9 us)
Sparse Core Ops, SparseCore 0:
  131.5 204.1 all-reduce.4
  338.2 95.7 all-reduce.6
